TPU v7x, 512 devices: a whole 4x4x16 slice. The times are simulated.
512 devices in a mesh: group: 32 (over x, z_hi, y), fsdp: 16 (over z_lo, core).
Axes of the slice: x: 4, y: 4, z: 16 (z_hi: 2, z_lo: 8; z = z_hi * 8 + z_lo), core: 2. Of those that a mesh axis runs over, the one named last changes fastest.
Arguments:
- inputs: bfloat16 [32, 2048, 8192], P('group', 'fsdp'), may hold values from -6 to 6
- teacher: bfloat16 [32, 2048, 512], P('group', 'fsdp'), may hold values from -6 to 6
- weight: bfloat16 [32, 8192, 512], P('group', 'fsdp'), may hold values from -6 to 6
- momentum: bfloat16 [32, 8192, 512], P('group', 'fsdp'), may hold values from -6 to 6
- exponent: int32 [4], replicated, may hold values from 0 to 4
Outputs:
- weight_mixed: bfloat16 [32, 8192, 512], P('group', 'fsdp')
- momentum_mixed: bfloat16 [32, 8192, 512], P('group', 'fsdp')
All inputs are finite; a program needn't handle non-finite values.
Results may differ from a plain program's by a relative error of at most 0.0073.
Values may be sent and summed in bfloat16 or wider, within the bound.
A program may use at most 64 MiB of HBM per device.

v0:
```python
import jax
import jax.numpy as jnp
from jax import lax
from jax.sharding import PartitionSpec as P

D = 8192
ROUNDS = 4


MIXES = (0.5, 0.4, 0.3, 0.2)


def shortened(x):

    def short(part):
        return part.astype(jnp.bfloat16) if part.dtype == jnp.float32 else part

    return jax.tree.map(short, x)


def swapped(x, axis, bit):
    return lax.ppermute(x, axis, [(i, i ^ 1 << bit) for i in range(lax.axis_size(axis))])


def exchange_with(level):

    def branch_fn(state):
        return jax.tree.map(
            lambda part, own: part.astype(own.dtype),
            swapped(shortened(state), "group", level),
            state,
        )

    return branch_fn


def per_device(inputs, teacher, weight, momentum, exponent):
    scale = D ** (-0.5)
    tokens = inputs[0]
    rows_local = weight[0]
    moment_local = momentum[0]
    columns = lax.all_to_all(tokens, "fsdp", split_axis=1, concat_axis=0, tiled=True)
    values = jnp.dot(
        tokens,
        lax.all_gather(rows_local, "fsdp", axis=0, tiled=True),
        preferred_element_type=jnp.float32,
    )
    error = (values * scale - teacher[0].astype(jnp.float32)).astype(jnp.bfloat16)
    grad = (
        lax.dot_general(
            columns,
            lax.all_gather(error, "fsdp", axis=0, tiled=True),
            (((0,), (0,)), ((), ())),
            preferred_element_type=jnp.float32,
        )
        * scale
    )
    moved = (0.9 * moment_local.astype(jnp.float32) + grad).astype(jnp.bfloat16)
    stepped = (rows_local.astype(jnp.float32) - 0.05 * moved.astype(jnp.float32)).astype(
        jnp.bfloat16
    )
    levels = lax.axis_size("group").bit_length() - 1
    branches = [exchange_with(level) for level in range(levels)]
    for rnd in range(ROUNDS):
        weight_c = MIXES[rnd]
        other_w, other_m = lax.switch(exponent[rnd], branches, (stepped, moved))
        stepped = (
            (1.0 - weight_c) * stepped.astype(jnp.float32) + weight_c * other_w.astype(jnp.float32)
        ).astype(jnp.bfloat16)
        moved = (
            (1.0 - weight_c) * moved.astype(jnp.float32) + weight_c * other_m.astype(jnp.float32)
        ).astype(jnp.bfloat16)
    return (stepped[None], moved[None])


def solution(mesh):
    return jax.shard_map(
        per_device,
        mesh=mesh,
        in_specs=(
            P("group", "fsdp", None),
            P("group", "fsdp", None),
            P("group", "fsdp", None),
            P("group", "fsdp", None),
            P(),
        ),
        out_specs=(P("group", "fsdp", None), P("group", "fsdp", None)),
        check_vma=False,
    )
```

profile of v0, /device:TPU:1, one launch (start us, length us, event | category | flops | bytes accessed | tf_op | source)
XLA Modules:
  0.0 568.1 jit_solution(13915217839260847118)
XLA Ops:
  7.9 4.1 copy.113
  12.0 14.2 %all-to-all-start = ((bf16[128,16,512]{0,2,1:T(8,128)(2,1)}), bf16[128,16,512]{0,2,1:T(8,128)(2,1)}, u32[]{:S(2)}, u32[]{:S(2)}) async-start(bf16[128,16,512]{0,2,1:T(8,128)(2,1)} %bitcast.46), calls=%async_computation | async-start | bytes 4194304 | tf_op jit(solution)/shard_map/all_to_all | solution.py:42
  26.3 174.5 %all-gather.6.cloned.1.call-done = bf16[1,8192,512]{2,1,0:T(8,128)(2,1)} async-done(((bf16[1,512,512]{2,1,0:T(8,128)(2,1)}), bf16[1,8192,512]{2,1,0:T(8,128)(2,1)}) %all-gather.6.cloned.1.call-update) | async-done | bytes 8388624 | tf_op jit(solution)/shard_map/all_gather | solution.py:45
  200.8 5.3 fusion.16
  209.8 3.9 copy.114
  213.7 96.0 %all-gather.4.cloned.1.call-done = bf16[2048,512]{1,0:T(8,128)(2,1)} async-done(((bf16[128,512]{1,0:T(8,128)(2,1)}), bf16[2048,512]{1,0:T(8,128)(2,1)}) %all-gather.4.cloned.1.call-update) | async-done | bytes 2097168 | tf_op jit(solution)/shard_map/all_gather | solution.py:52
  309.7 3.6 fusion.22
  313.3 26.3 %conditional.12 = (f32[512,512]{0,1:T(8,128)S(1)}, f32[512,512]{0,1:T(8,128)}) conditional(s32[]{:T(128)} %bitcast.9, (bf16[512,512]{0,1:T(8,128)(2,1)S(1)}, bf16[512,512]{0,1:T(8,128)(2,1)S(1)}) %fusion.22, (bf16[512,512]{0,1:T(8,128)(2,1)S(1)}, bf16[512,512]{0,1:T(8,128)(2,1)S(1)}) %fusion.22, ...), branch_computations={%region_0.0_spmd, %region_1.0_spmd, %region_2.0_spmd, %region_3.0_... | conditional | bytes 9437280
  313.5 2.9 collective-permute-start
  319.8 7.3 %collective-permute-done = bf16[512,512]{1,0:T(8,128)(2,1)S(1)} collective-permute-done((bf16[512,512]{1,0:T(8,128)(2,1)S(1)}, bf16[512,512]{1,0:T(8,128)(2,1)S(1)}, u32[]{:S(2)}, u32[]{:S(2)}) %collective-permute-start) | collective-permute-done | bytes 524320 | tf_op jit(solution)/shard_map/cond/branch_0_fun/ppermute | solution.py:22
  327.3 11.0 %collective-permute-done.1 = bf16[512,512]{1,0:T(8,128)(2,1)S(1)} collective-permute-done((bf16[512,512]{1,0:T(8,128)(2,1)}, bf16[512,512]{1,0:T(8,128)(2,1)S(1)}, u32[]{:S(2)}, u32[]{:S(2)}) %collective-permute-start.1) | collective-permute-done | bytes 524320 | tf_op jit(solution)/shard_map/cond/branch_0_fun/ppermute | solution.py:22
  341.2 28.3 %conditional.13 = (f32[512,512]{0,1:T(8,128)S(1)}, f32[512,512]{0,1:T(8,128)S(1)}) conditional(s32[]{:T(128)} %bitcast.10, (bf16[512,512]{0,1:T(8,128)(2,1)S(1)}, bf16[512,512]{0,1:T(8,128)(2,1)S(1)}) %tuple.217, (bf16[512,512]{0,1:T(8,128)(2,1)S(1)}, bf16[512,512]{0,1:T(8,128)(2,1)S(1)}) %tuple.217, ...), branch_computations={%region_5.0_spmd, %region_6.0_spmd, %region_7.0_spmd, %region_8.0_... | conditional | bytes 9437280
  341.6 5.4 collective-permute-start.18
  349.2 7.7 %collective-permute-done.18 = bf16[512,512]{1,0:T(8,128)(2,1)S(1)} collective-permute-done((bf16[512,512]{1,0:T(8,128)(2,1)S(1)}, bf16[512,512]{1,0:T(8,128)(2,1)S(1)}, u32[]{:S(2)}, u32[]{:S(2)}) %collective-permute-start.18) | collective-permute-done | bytes 524320 | tf_op jit(solution)/shard_map/cond/branch_4_fun/ppermute | solution.py:22
  357.1 11.1 %collective-permute-done.19 = bf16[512,512]{1,0:T(8,128)(2,1)} collective-permute-done((bf16[512,512]{1,0:T(8,128)(2,1)S(1)}, bf16[512,512]{1,0:T(8,128)(2,1)}, u32[]{:S(2)}, u32[]{:S(2)}) %collective-permute-start.19) | collective-permute-done | bytes 524320 | tf_op jit(solution)/shard_map/cond/branch_4_fun/ppermute | solution.py:22
  371.9 88.0 %conditional.14 = (f32[512,512]{0,1:T(8,128)S(1)}, f32[512,512]{0,1:T(8,128)}) conditional(s32[]{:T(128)} %bitcast.11, (bf16[512,512]{0,1:T(8,128)(2,1)S(1)}, bf16[512,512]{0,1:T(8,128)(2,1)S(1)}) %tuple.218, (bf16[512,512]{0,1:T(8,128)(2,1)S(1)}, bf16[512,512]{0,1:T(8,128)(2,1)S(1)}) %tuple.218, ...), branch_computations={%region_10.0_spmd, %region_11.0_spmd, %region_12.0_spmd, %region_1... | conditional | bytes 9437280
  375.1 12.1 %collective-permute-start.25 = (bf16[512,512]{1,0:T(8,128)(2,1)}, bf16[512,512]{1,0:T(8,128)(2,1)S(1)}, u32[]{:S(2)}, u32[]{:S(2)}) collective-permute-start(bf16[512,512]{1,0:T(8,128)(2,1)} %copy.144), channel_id=1, source_target_pairs={{0,64},{16,80},{32,96},{48,112},{64,0},{80,16},{96,32},{112,48},{1... | collective-permute-start | bytes 1572872 | tf_op jit(solution)/shard_map/cond/branch_2_fun/ppermute | solution.py:22
  387.2 60.2 %collective-permute-done.24 = bf16[512,512]{1,0:T(8,128)(2,1)S(1)} collective-permute-done((bf16[512,512]{1,0:T(8,128)(2,1)S(1)}, bf16[512,512]{1,0:T(8,128)(2,1)S(1)}, u32[]{:S(2)}, u32[]{:S(2)}) %collective-permute-start.24) | collective-permute-done | bytes 524320 | tf_op jit(solution)/shard_map/cond/branch_2_fun/ppermute | solution.py:22
  447.6 11.1 %collective-permute-done.25 = bf16[512,512]{1,0:T(8,128)(2,1)S(1)} collective-permute-done((bf16[512,512]{1,0:T(8,128)(2,1)}, bf16[512,512]{1,0:T(8,128)(2,1)S(1)}, u32[]{:S(2)}, u32[]{:S(2)}) %collective-permute-start.25) | collective-permute-done | bytes 524320 | tf_op jit(solution)/shard_map/cond/branch_2_fun/ppermute | solution.py:22
  461.3 95.8 %conditional.15 = (f32[512,512]{0,1:T(8,128)S(1)}, f32[512,512]{0,1:T(8,128)S(1)}) conditional(s32[]{:T(128)} %bitcast.12, (bf16[512,512]{0,1:T(8,128)(2,1)S(1)}, bf16[512,512]{0,1:T(8,128)(2,1)S(1)}) %tuple.219, (bf16[512,512]{0,1:T(8,128)(2,1)S(1)}, bf16[512,512]{0,1:T(8,128)(2,1)S(1)}) %tuple.219, ...), branch_computations={%region_15.0_spmd, %region_16.0_spmd, %region_17.0_spmd, %region_1... | conditional | bytes 9437280
  461.5 9.6 %collective-permute-start.34 = (bf16[512,512]{1,0:T(8,128)(2,1)S(1)}, bf16[512,512]{1,0:T(8,128)(2,1)S(1)}, u32[]{:S(2)}, u32[]{:S(2)}) collective-permute-start(bf16[512,512]{1,0:T(8,128)(2,1)S(1)} %copy.155), channel_id=1, source_target_pairs={{0,64},{16,80},{32,96},{48,112},{64,0},{80,16},{96,32},{112,48},{1... | collective-permute-start | bytes 1572872 | tf_op jit(solution)/shard_map/cond/branch_2_fun/ppermute | solution.py:22
  471.3 4.4 collective-permute-start.35
  475.8 68.7 %collective-permute-done.34 = bf16[512,512]{1,0:T(8,128)(2,1)S(1)} collective-permute-done((bf16[512,512]{1,0:T(8,128)(2,1)S(1)}, bf16[512,512]{1,0:T(8,128)(2,1)S(1)}, u32[]{:S(2)}, u32[]{:S(2)}) %collective-permute-start.34) | collective-permute-done | bytes 524320 | tf_op jit(solution)/shard_map/cond/branch_2_fun/ppermute | solution.py:22
  544.7 11.1 %collective-permute-done.35 = bf16[512,512]{1,0:T(8,128)(2,1)} collective-permute-done((bf16[512,512]{1,0:T(8,128)(2,1)S(1)}, bf16[512,512]{1,0:T(8,128)(2,1)}, u32[]{:S(2)}, u32[]{:S(2)}) %collective-permute-start.35) | collective-permute-done | bytes 524320 | tf_op jit(solution)/shard_map/cond/branch_2_fun/ppermute | solution.py:22
  (52 shorter events, 26.8 us)
Async XLA Ops:
  7.2 193.6 %all-gather.6.cloned.1.call-start = ((), (), s32[]{:S(2)}) async-start(), calls=%async_computation.2 | async-start | bytes 8912896 | tf_op jit(solution)/shard_map/all_gather | solution.py:45
  12.0 188.8 %copy-start = (bf16[1,128,8192]{2,1,0:T(8,128)(2,1)S(1)}, bf16[1,128,8192]{2,1,0:T(8,128)(2,1)}, u32[]{:S(2)}) copy-start(bf16[1,128,8192]{2,1,0:T(8,128)(2,1)} %param.25) | copy-start | bytes 6291460
  12.0 188.8 %copy-start.6 = (bf16[1,128,512]{2,1,0:T(8,128)(2,1)S(1)}, bf16[1,128,512]{2,1,0:T(8,128)(2,1)}, u32[]{:S(2)}) copy-start(bf16[1,128,512]{2,1,0:T(8,128)(2,1)} %param.26) | copy-start | bytes 393220
  12.0 197.7 %all-to-all-start = ((bf16[128,16,512]{0,2,1:T(8,128)(2,1)}), bf16[128,16,512]{0,2,1:T(8,128)(2,1)}, u32[]{:S(2)}, u32[]{:S(2)}) async-start(bf16[128,16,512]{0,2,1:T(8,128)(2,1)} %bitcast.46), calls=%async_computation | async-start | bytes 4194304 | tf_op jit(solution)/shard_map/all_to_all | solution.py:42
  26.2 179.9 %copy-start.4 = (bf16[1,512,512]{2,1,0:T(8,128)(2,1)S(1)}, bf16[1,512,512]{2,1,0:T(8,128)(2,1)}, u32[]{:S(2)}) copy-start(bf16[1,512,512]{2,1,0:T(8,128)(2,1)} %param.27) | copy-start | bytes 1572868
  26.2 180.2 %copy-start.7 = (s32[4]{0:T(128)S(1)}, s32[4]{0:T(128)}, u32[]{:S(2)}) copy-start(s32[4]{0:T(128)} %param.29) | copy-start | bytes 52
  26.2 183.3 %copy-start.5 = (bf16[1,512,512]{2,1,0:T(8,128)(2,1)S(1)}, bf16[1,512,512]{2,1,0:T(8,128)(2,1)}, u32[]{:S(2)}) copy-start(bf16[1,512,512]{2,1,0:T(8,128)(2,1)} %param.28) | copy-start | bytes 1572868
  26.2 283.5 %all-gather.4.cloned.1.call-start = ((), (), s32[]{:S(2)}) async-start(), calls=%async_computation.1 | async-start | bytes 2228224 | tf_op jit(solution)/shard_map/all_gather | solution.py:52
  313.5 13.6 %collective-permute-start = (bf16[512,512]{1,0:T(8,128)(2,1)S(1)}, bf16[512,512]{1,0:T(8,128)(2,1)S(1)}, u32[]{:S(2)}, u32[]{:S(2)}) collective-permute-start(bf16[512,512]{1,0:T(8,128)(2,1)S(1)} %copy.115), channel_id=1, source_target_pairs={{0,16},{16,0},{32,48},{48,32},{64,80},{80,64},{96,112},{112,96},{1... | collective-permute-start | bytes 1572872 | tf_op jit(solution)/shard_map/cond/branch_0_fun/ppermute | solution.py:22
  317.5 20.9 %collective-permute-start.1 = (bf16[512,512]{1,0:T(8,128)(2,1)}, bf16[512,512]{1,0:T(8,128)(2,1)S(1)}, u32[]{:S(2)}, u32[]{:S(2)}) collective-permute-start(bf16[512,512]{1,0:T(8,128)(2,1)} %copy.116), channel_id=1, source_target_pairs={{0,16},{16,0},{32,48},{48,32},{64,80},{80,64},{96,112},{112,96},{1... | collective-permute-start | bytes 1572872 | tf_op jit(solution)/shard_map/cond/branch_0_fun/ppermute | solution.py:22
  341.6 15.3 %collective-permute-start.18 = (bf16[512,512]{1,0:T(8,128)(2,1)S(1)}, bf16[512,512]{1,0:T(8,128)(2,1)S(1)}, u32[]{:S(2)}, u32[]{:S(2)}) collective-permute-start(bf16[512,512]{1,0:T(8,128)(2,1)S(1)} %copy.135), channel_id=1, source_target_pairs={{0,256},{16,272},{32,288},{48,304},{64,320},{80,336},{96,352},{112... | collective-permute-start | bytes 1572872 | tf_op jit(solution)/shard_map/cond/branch_4_fun/ppermute | solution.py:22
  347.2 21.0 %collective-permute-start.19 = (bf16[512,512]{1,0:T(8,128)(2,1)S(1)}, bf16[512,512]{1,0:T(8,128)(2,1)}, u32[]{:S(2)}, u32[]{:S(2)}) collective-permute-start(bf16[512,512]{1,0:T(8,128)(2,1)S(1)} %copy.136), channel_id=1, source_target_pairs={{0,256},{16,272},{32,288},{48,304},{64,320},{80,336},{96,352},{112... | collective-permute-start | bytes 1572872 | tf_op jit(solution)/shard_map/cond/branch_4_fun/ppermute | solution.py:22
  369.5 1.0 copy-start.1
  370.5 1.2 copy-start.2
  372.1 75.2 %collective-permute-start.24 = (bf16[512,512]{1,0:T(8,128)(2,1)S(1)}, bf16[512,512]{1,0:T(8,128)(2,1)S(1)}, u32[]{:S(2)}, u32[]{:S(2)}) collective-permute-start(bf16[512,512]{1,0:T(8,128)(2,1)S(1)} %copy.143), channel_id=1, source_target_pairs={{0,64},{16,80},{32,96},{48,112},{64,0},{80,16},{96,32},{112,48},{1... | collective-permute-start | bytes 1572872 | tf_op jit(solution)/shard_map/cond/branch_2_fun/ppermute | solution.py:22
  375.1 83.6 %collective-permute-start.25 = (bf16[512,512]{1,0:T(8,128)(2,1)}, bf16[512,512]{1,0:T(8,128)(2,1)S(1)}, u32[]{:S(2)}, u32[]{:S(2)}) collective-permute-start(bf16[512,512]{1,0:T(8,128)(2,1)} %copy.144), channel_id=1, source_target_pairs={{0,64},{16,80},{32,96},{48,112},{64,0},{80,16},{96,32},{112,48},{1... | collective-permute-start | bytes 1572872 | tf_op jit(solution)/shard_map/cond/branch_2_fun/ppermute | solution.py:22
  459.9 1.2 copy-start.3
  461.5 82.9 %collective-permute-start.34 = (bf16[512,512]{1,0:T(8,128)(2,1)S(1)}, bf16[512,512]{1,0:T(8,128)(2,1)S(1)}, u32[]{:S(2)}, u32[]{:S(2)}) collective-permute-start(bf16[512,512]{1,0:T(8,128)(2,1)S(1)} %copy.155), channel_id=1, source_target_pairs={{0,64},{16,80},{32,96},{48,112},{64,0},{80,16},{96,32},{112,48},{1... | collective-permute-start | bytes 1572872 | tf_op jit(solution)/shard_map/cond/branch_2_fun/ppermute | solution.py:22
  471.3 84.5 %collective-permute-start.35 = (bf16[512,512]{1,0:T(8,128)(2,1)S(1)}, bf16[512,512]{1,0:T(8,128)(2,1)}, u32[]{:S(2)}, u32[]{:S(2)}) collective-permute-start(bf16[512,512]{1,0:T(8,128)(2,1)S(1)} %copy.156), channel_id=1, source_target_pairs={{0,64},{16,80},{32,96},{48,112},{64,0},{80,16},{96,32},{112,48},{1... | collective-permute-start | bytes 1572872 | tf_op jit(solution)/shard_map/cond/branch_2_fun/ppermute | solution.py:22
Sparse Core Ops, SparseCore 0:
  10.1 190.6 all-gather.5
  206.3 103.3 all-gather.3
where the time goes:
time: 569 us; the launch traced here: 568 us
  waiting for transfers between devices  459 us (81%)
  starting transfers between devices  54.8 us (10%)
  local copies, waits for them, and re-layouts  24.4 us (4%)
  between operations  16.6 us (3%)
  matrix products  8.9 us (2%)
    ppermute x8, waiting for transfers between devices, swapped(): lax.ppermute(x, axis, [(i, i ^ 1 << bit) for i in range(lax.axis_size(axi...  188 us
    all_gather x1, waiting for transfers between devices, per_device(): lax.all_gather(rows_local, 'fsdp', axis=0, tiled=True)  175 us
    all_gather x1, waiting for transfers between devices, per_device(): lax.all_gather(error, 'fsdp', axis=0, tiled=True)  96 us
    ppermute x8, starting transfers between devices, swapped(): lax.ppermute(x, axis, [(i, i ^ 1 << bit) for i in range(lax.axis_size(axi...  40.6 us
    all_to_all x1, starting transfers between devices, per_device(): lax.all_to_all(tokens, 'fsdp', split_axis=1, concat_axis=0, tiled=True)  14.2 us
  transfers between devices with their start and end apart: 11, of which 10 were waited for; matrix products, arithmetic and copies ran while one was open for 3% of the time, Pallas kernels for 0%

commit v1 on v0

v1 whole, which is shorter than its diff:
```python
import functools

import jax
import jax.numpy as jnp
from jax import lax
from jax.experimental import pallas as pl
from jax.experimental.pallas import tpu as pltpu
from jax.sharding import PartitionSpec as P

D = 8192
KV = 512
ROUNDS = 4
MIXES = (0.5, 0.4, 0.3, 0.2)
MESH = pl.DeviceIdType.MESH
F32 = jnp.float32
BF16 = jnp.bfloat16

CHIPS = 8
DEVS = 16
TOK = 128
ROWS = 512
HALF = KV // 2
QW = 128
ITEM = 256
NT = DEVS * TOK // ITEM
NITEM = NT * HALF // QW
SKEW = 2

ORDERS = (("y", 0), ("y", 1), ("x", 0), ("x", 1))
BITS = {"y": (1, 3), "x": (8, 24)}


def blocks(rows, step, body):
    def one(i, carry):
        body(pl.ds(pl.multiple_of(i * step, step), step))
        return carry

    lax.fori_loop(0, rows // step, one, 0)


class Mix:
    def __init__(self, raw, acc, send, recv, ssem, rsem, coef, step):
        self.raw, self.acc, self.send, self.recv = raw, acc, send, recv
        self.ssem, self.rsem, self.coef, self.step = ssem, rsem, coef, step
        self.size = raw.shape[0] // 4

    def axis_of(self, k, stage):
        first, order = ORDERS[k]
        axis = first if stage < 2 else ("x" if first == "y" else "y")
        return axis, order

    def factors(self, k, stage):
        axis, order = self.axis_of(k, stage)
        base = (0 if axis == "y" else 8) + 4 * order
        return [self.coef[base + i] for i in range(4)]

    def copy(self, k, stage):
        axis, order = self.axis_of(k, stage)
        bit = BITS[axis][order if stage % 2 == 0 else 1 - order]
        rows = pl.ds(k * self.size, self.size)
        src = self.raw.at[rows] if stage == 0 else self.send.at[stage - 1, rows]
        return pltpu.make_async_remote_copy(
            src_ref=src,
            dst_ref=self.recv.at[stage, rows],
            send_sem=self.ssem.at[k, stage],
            recv_sem=self.rsem.at[k, stage],
            device_id={"group": lax.axis_index("group") ^ bit},
            device_id_type=MESH,
        )

    def begin(self, k):
        self.copy(k, 0).start()

    def advance(self, k, stage):
        self.copy(k, stage - 1).wait_recv()
        if stage in (1, 3):
            s_own, s_got, o_own, o_got = self.factors(k, stage)

        def body(rows):
            at = pl.ds(k * self.size + rows.start, self.step)
            got = self.recv[stage - 1, at].astype(F32)
            if stage == 1:
                own = self.raw[at].astype(F32)
            else:
                own = self.acc[at]
            if stage in (1, 3):
                self.send[stage - 1, at] = (s_own * own + s_got * got).astype(BF16)
                self.acc[at] = o_own * own + o_got * got
            else:
                total = own + got
                self.acc[at] = total
                if stage == 2:
                    self.send[1, at] = total.astype(BF16)

        blocks(self.size, self.step, body)
        if stage < 4:
            self.copy(k, stage).start()

    def drain(self):
        for k in range(4):
            for stage in range(4):
                self.copy(k, stage).wait_send()


def step_kernel(
    coef, inputs, teacher, weight, momentum, out_w, out_m,
    xc, wm, tc, wm_acc, wm_send, wm_recv, part, right_in, left_in, right_out, left_out,
    gt, g_raw, g_acc, g_send, g_recv, fin,
    a2a_s, a2a_r, fwd_s, fwd_r, own_s, sib_s, sib_r, wm_ss, wm_rs, g_ss, g_rs,
    rs_s, rs_r, ls_s, ls_r, fin_l, fin_s, fin_r,
):
    group, f = lax.axis_index("group"), lax.axis_index("fsdp")
    z, c = f // 2, f % 2
    scale = D ** (-0.5)

    barrier = pltpu.get_barrier_semaphore()

    def greet(i, carry):
        pl.semaphore_signal(
            barrier, inc=1, device_id={"fsdp": (f + i) % DEVS}, device_id_type=MESH
        )
        return carry

    lax.fori_loop(1, DEVS, greet, 0)
    for bit in BITS["y"] + BITS["x"]:
        pl.semaphore_signal(
            barrier, inc=1, device_id={"group": group ^ bit}, device_id_type=MESH
        )
    pl.semaphore_wait(barrier, DEVS - 1 + 4)

    def to_sibling(src, dst, s, r):
        return pltpu.make_async_remote_copy(
            src_ref=src, dst_ref=dst, send_sem=s, recv_sem=r,
            device_id={"fsdp": f ^ 1}, device_id_type=MESH,
        )

    mine = pl.ds(pl.multiple_of(c * HALF, HALF), HALF)
    other = pl.ds(pl.multiple_of((1 - c) * HALF, HALF), HALF)
    w_rows = pl.ds(pl.multiple_of(c * ROWS, ROWS), ROWS)
    m_rows = pl.ds(pl.multiple_of(2 * ROWS + c * ROWS, ROWS), ROWS)
    t_rows = pl.ds(pl.multiple_of(c * TOK, TOK), TOK)
    x_rows = pl.ds(pl.multiple_of(f * TOK, TOK), TOK)
    x_cols = pl.ds(pl.multiple_of(z * 2 * ROWS, 2 * ROWS), 2 * ROWS)
    shared = (
        (weight, mine, other, wm, w_rows),
        (momentum, mine, other, wm, m_rows),
        (teacher, mine, other, tc, t_rows),
        (inputs, x_cols, x_cols, xc, x_rows),
    )
    local = [
        pltpu.make_async_copy(src.at[0, :, keep], dst.at[rows], own_s.at[i])
        for i, (src, keep, _, dst, rows) in enumerate(shared)
    ]
    across = [
        to_sibling(src.at[0, :, give], dst.at[rows], sib_s.at[i], sib_r.at[i])
        for i, (src, _, give, dst, rows) in enumerate(shared)
    ]
    for i in range(2):
        local[i].start()
        across[i].start()

    def far_device(i, ahead):
        return (z + ahead) % CHIPS * 2 + i % 2

    def block(i, there):
        dev = far_device(i, i // 2 if there else CHIPS - i // 2)
        to = dev if there else f
        of = f if there else dev
        return dev, pltpu.make_async_remote_copy(
            src_ref=inputs.at[0, :, pl.ds(pl.multiple_of(to * ROWS, ROWS), ROWS)],
            dst_ref=xc.at[
                pl.ds(pl.multiple_of(of * TOK, TOK), TOK),
                pl.ds(pl.multiple_of((to % 2) * ROWS, ROWS), ROWS),
            ],
            send_sem=a2a_s.at[i],
            recv_sem=a2a_r.at[of],
            device_id={"fsdp": dev},
            device_id_type=MESH,
        )

    def send_block(i, carry):
        block(i, True)[1].start()
        return carry

    lax.fori_loop(2, DEVS, send_block, 0)
    for i in range(2, 4):
        local[i].start()
        across[i].start()

    def zeros(ref):
        ref[...] = jnp.zeros_like(ref)

    pl.when(z == 0)(lambda: zeros(right_in))
    pl.when(z == CHIPS - 1)(lambda: zeros(left_in))
    zeros(gt)

    for i in range(2):
        local[i].wait()
        across[i].wait()
    mix = Mix(wm, wm_acc, wm_send, wm_recv, wm_ss, wm_rs, coef, 64)
    for k in range(4):
        mix.begin(k)
    for stage in range(1, 5):
        for k in range(4):
            mix.advance(k, stage)
    mix.drain()
    for i in range(2, 4):
        local[i].wait()
        across[i].wait()

    def forward(j, cols):
        at = (pl.ds(pl.multiple_of(j * TOK, TOK), TOK), pl.ds(pl.multiple_of(cols * ROWS, ROWS), ROWS))
        return to_sibling(xc.at[at], xc.at[at], fwd_s.at[j], fwd_r.at[j])

    def pass_on(i, carry):
        dev, arrival = block(i, False)
        arrival.wait_recv()
        forward(dev, c).start()
        return carry

    lax.fori_loop(2, DEVS, pass_on, 0)

    def settle(i, carry):
        dev = far_device(i, CHIPS - i // 2)
        forward(dev, c).wait_send()
        forward(dev, 1 - c).wait_recv()
        block(i, True)[1].wait_send()
        return carry

    lax.fori_loop(2, DEVS, settle, 0)

    def share(t, carry):
        rows = pl.ds(pl.multiple_of(t * ITEM, ITEM), ITEM)
        own = jnp.dot(xc[rows], wm[: 2 * ROWS], preferred_element_type=F32) * scale
        for q in range(HALF // QW):
            part[q * NT + t] = own[:, q * QW : (q + 1) * QW]
        return carry

    lax.fori_loop(0, NT, share, 0)
    per_chip = 2 * TOK // ITEM
    for q in range(HALF // QW):
        for i in range(per_chip):
            n = q * NT + z * per_chip + i
            part[n] = part[n] - tc[i * ITEM : (i + 1) * ITEM, q * QW : (q + 1) * QW].astype(F32)

    def hop(n, out, into, s, r, by):
        return pltpu.make_async_remote_copy(
            src_ref=out.at[n], dst_ref=into.at[n], send_sem=s.at[n], recv_sem=r.at[n],
            device_id={"fsdp": (f + DEVS + 2 * by) % DEVS}, device_id_type=MESH,
        )

    def to_right(n):
        return hop(n, right_out, right_in, rs_s, rs_r, 1)

    def to_left(n):
        return hop(n, left_out, left_in, ls_s, ls_r, -1)

    def travel(n, copy, into, out, first, last):
        @pl.when(jnp.logical_and(n >= 0, n < NITEM))
        def _():
            @pl.when(jnp.logical_not(first))
            def _():
                copy(n).wait_recv()

            @pl.when(jnp.logical_not(last))
            def _():
                out[n] = (part[n] + into[n].astype(F32)).astype(BF16)
                copy(n).start()

    far = jnp.maximum(z, CHIPS - 1 - z)

    def step(s, carry):
        travel(s - SKEW * z, to_right, right_in, right_out, z == 0, z == CHIPS - 1)
        travel(s - SKEW * (CHIPS - 1 - z), to_left, left_in, left_out, z == CHIPS - 1, z == 0)
        n = s - SKEW * far

        @pl.when(jnp.logical_and(n >= 0, n < NITEM))
        def _():
            error = (part[n] + right_in[n].astype(F32) + left_in[n].astype(F32)).astype(BF16)
            q, t = n // NT, n % NT
            rows = pl.ds(pl.multiple_of(t * ITEM, ITEM), ITEM)
            gt[q] += lax.dot_general(
                error, xc[rows], (((0,), (0,)), ((), ())), preferred_element_type=F32
            )

        return carry

    lax.fori_loop(0, NITEM + SKEW * (CHIPS - 1), step, 0)

    def sent(n, carry):
        pl.when(z < CHIPS - 1)(lambda: to_right(n).wait_send())
        pl.when(z > 0)(lambda: to_left(n).wait_send())
        return carry

    lax.fori_loop(0, NITEM, sent, 0)

    for q in range(HALF // QW):
        g_raw[:, q * QW : (q + 1) * QW] = (gt[q] * scale).T.astype(BF16)
    mix = Mix(g_raw, g_acc, g_send, g_recv, g_ss, g_rs, coef, 64)
    for k in range(4):
        mix.begin(k)
    for stage in range(1, 5):
        for k in range(4):
            mix.advance(k, stage)

    def finish(rows):
        moved = 0.9 * wm_acc[pl.ds(2 * ROWS + rows.start, 64)] + g_acc[rows]
        fin[1, rows] = moved.astype(BF16)
        fin[0, rows] = (wm_acc[rows] - 0.05 * moved).astype(BF16)

    blocks(2 * ROWS, 64, finish)
    o_rows = pl.ds(pl.multiple_of((1 - c) * ROWS, ROWS), ROWS)
    ends = []
    for i, out in enumerate((out_w, out_m)):
        ends.append(to_sibling(fin.at[i, o_rows], out.at[0, :, mine], fin_s.at[i], fin_r.at[i]))
        ends.append(pltpu.make_async_copy(fin.at[i, w_rows], out.at[0, :, mine], fin_l.at[i]))
    for copy in ends:
        copy.start()
    mix.drain()
    for copy in ends:
        copy.wait()


def step_call(coef, inputs, teacher, weight, momentum):
    dma = lambda *n: pltpu.SemaphoreType.DMA(n)
    anywhere = pl.BlockSpec(memory_space=pl.ANY)
    shape = jax.ShapeDtypeStruct((1, ROWS, KV), BF16)
    rows = 2 * ROWS
    return pl.pallas_call(
        step_kernel,
        name="step",
        out_shape=(shape, shape),
        in_specs=[pl.BlockSpec(memory_space=pltpu.SMEM)] + [anywhere] * 4,
        out_specs=(anywhere, anywhere),
        scratch_shapes=[
            pltpu.VMEM((DEVS * TOK, rows), BF16),
            pltpu.VMEM((2 * rows, HALF), BF16),
            pltpu.VMEM((2 * TOK, HALF), BF16),
            pltpu.VMEM((2 * rows, HALF), F32),
            pltpu.VMEM((3, 2 * rows, HALF), BF16),
            pltpu.VMEM((4, 2 * rows, HALF), BF16),
            pltpu.VMEM((NITEM, ITEM, QW), F32),
            pltpu.VMEM((NITEM, ITEM, QW), BF16),
            pltpu.VMEM((NITEM, ITEM, QW), BF16),
            pltpu.VMEM((NITEM, ITEM, QW), BF16),
            pltpu.VMEM((NITEM, ITEM, QW), BF16),
            pltpu.VMEM((HALF // QW, QW, rows), F32),
            pltpu.VMEM((rows, HALF), BF16),
            pltpu.VMEM((rows, HALF), F32),
            pltpu.VMEM((3, rows, HALF), BF16),
            pltpu.VMEM((4, rows, HALF), BF16),
            pltpu.VMEM((2, rows, HALF), BF16),
            dma(DEVS), dma(DEVS), dma(DEVS), dma(DEVS),
            dma(4), dma(4), dma(4),
            dma(4, 4), dma(4, 4), dma(4, 4), dma(4, 4),
            dma(NITEM), dma(NITEM), dma(NITEM), dma(NITEM),
            dma(2), dma(2), dma(2),
        ],
        compiler_params=pltpu.CompilerParams(
            collective_id=0, has_side_effects=True, vmem_limit_bytes=56 * 2**20
        ),
    )(coef, inputs, teacher, weight, momentum)


def far_kernel(parts, factor, a_ref, b_ref, oa_ref, ob_ref, got, ss, rs):
    partner = lax.axis_index("group") ^ 4
    barrier = pltpu.get_barrier_semaphore()
    pl.semaphore_signal(barrier, inc=1, device_id={"group": partner}, device_id_type=MESH)
    pl.semaphore_wait(barrier, 1)
    size = ROWS // parts
    copies = []
    for i, ref in enumerate((a_ref, b_ref)):
        for j in range(parts):
            rows = pl.ds(j * size, size)
            copies.append(
                pltpu.make_async_remote_copy(
                    src_ref=ref.at[0, rows], dst_ref=got.at[i, rows],
                    send_sem=ss.at[i * parts + j], recv_sem=rs.at[i * parts + j],
                    device_id={"group": partner}, device_id_type=MESH,
                )
            )
            copies[-1].start()
    own, far = factor[0], factor[1]
    for i, (ref, out) in enumerate(((a_ref, oa_ref), (b_ref, ob_ref))):
        for j in range(parts):
            copies[i * parts + j].wait()

            def body(rows):
                at = pl.ds(j * size + rows.start, 64)
                out[0, at] = (own * ref[0, at].astype(F32) + far * got[i, at].astype(F32)).astype(BF16)

            blocks(size, 64, body)


def far_call(factor, a, b):
    parts = 2
    shape = jax.ShapeDtypeStruct((1, ROWS, KV), BF16)
    vmem = pl.BlockSpec(memory_space=pltpu.VMEM)
    return pl.pallas_call(
        functools.partial(far_kernel, parts),
        name="far",
        out_shape=(shape, shape),
        in_specs=[pl.BlockSpec(memory_space=pltpu.SMEM), vmem, vmem],
        out_specs=(vmem, vmem),
        scratch_shapes=[
            pltpu.VMEM((2, ROWS, KV), BF16),
            pltpu.SemaphoreType.DMA((2 * parts,)),
            pltpu.SemaphoreType.DMA((2 * parts,)),
        ],
        compiler_params=pltpu.CompilerParams(
            collective_id=1, has_side_effects=True, vmem_limit_bytes=24 * 2**20
        ),
    )(factor, a, b)


def per_device(inputs, teacher, weight, momentum, exponent):
    levels = jnp.arange(5, dtype=jnp.int32)
    keep = jnp.asarray([1.0 - 2.0 * m for m in MIXES], F32)
    left = jnp.prod(jnp.where(exponent[None, :] == levels[:, None], keep[None, :], 1.0), axis=1)
    own, far = (1.0 + left) * 0.5, (1.0 - left) * 0.5
    coef = []
    for low, high in ((0, 1), (3, 4)):
        a0, b0, a1, b1 = own[low], far[low], own[high], far[high]
        coef += [b0 * b1, a0 * b1, a0 * a1, b0 * a1]
        coef += [b0 * a1, a0 * b1, a0 * a1, b0 * b1]
    pair = step_call(jnp.stack(coef), inputs, teacher, weight, momentum)
    factor = jnp.stack([own[2], far[2]])
    return lax.cond(
        jnp.any(exponent == 2),
        lambda a, b: tuple(far_call(factor, a, b)),
        lambda a, b: (a, b),
        *pair,
    )


def solution(mesh):
    return jax.shard_map(
        per_device,
        mesh=mesh,
        in_specs=(
            P("group", "fsdp", None),
            P("group", "fsdp", None),
            P("group", "fsdp", None),
            P("group", "fsdp", None),
            P(),
        ),
        out_specs=(P("group", "fsdp", None), P("group", "fsdp", None)),
        check_vma=False,
    )
```

time: 569 us -> 301 us (0.53)
  the two profiles are of different devices: /device:TPU:1 before, /device:TPU:65 now
where the time goes in v1:
time: 301 us
  Pallas kernels  283 us (94%)
  between operations  11 us (4%)
  other arithmetic  3.47 us (1%)
    pallas_call x1, Pallas kernels, step_call(): pl.pallas_call(step_kernel, name='step', out_shape=(shape, shape), in_spe...  181 us
    pallas_call x1, Pallas kernels, far_call(): pl.pallas_call(functools.partial(far_kernel, parts), name='far', out_shap...  102 us

profile of v1, /device:TPU:65, one launch (start us, length us, event | category | flops | bytes accessed | tf_op | source)
XLA Modules:
  0.0 300.6 jit_solution(11108584191549395524)
XLA Ops:
  0.6 1.3 compare_reduce_fusion
  2.6 0.8 select_reduce_fusion
  3.3 0.7 fusion
  13.8 0.6 stack.4.coef
  14.4 1.4 pad_maximum_fusion
  15.8 180.6 %step.1 = (bf16[1,512,512]{2,1,0:T(8,128)(2,1)S(1)}, bf16[1,512,512]{2,1,0:T(8,128)(2,1)S(1)}) custom-call(f32[16]{0:T(128)} %stack.4.coef, bf16[1,128,8192]{2,1,0:T(8,128)(2,1)} %inputs.1, bf16[1,128,512]{2,1,0:T(8,128)(2,1)} %teacher.1, bf16[1,512,512]{2,1,0:T(8,128)(2,1)} %weight.1, bf16[1,512,512]{2,1,0:T(8,128)(2,1)} %momentum.1), custom_call_target="tpu_custom_call" | custom-call | tf_op jit(solution)/shard_map/step/pallas_call | solution.py:329
  196.4 102.6 %conditional.1 = ((bf16[1,512,512]{2,1,0:T(8,128)(2,1)S(1)}, bf16[1,512,512]{2,1,0:T(8,128)(2,1)S(1)})) conditional(s32[]{:T(128)} %convert_element_type.3, (bf16[1,512,512]{2,1,0:T(8,128)(2,1)S(1)}, bf16[1,512,512]{2,1,0:T(8,128)(2,1)S(1)}) %step.1, (f32[2]{0:T(128)S(1)}, bf16[1,512,512]{2,1,0:T(8,128)(2,1)S(1)}, ...), branch_computations={%region_2.3_spmd, %region_3.4_spmd} | conditional | bytes 2097160 | solution.py:428
  196.5 102.5 %far.1 = (bf16[1,512,512]{2,1,0:T(8,128)(2,1)S(1)}, bf16[1,512,512]{2,1,0:T(8,128)(2,1)S(1)}) custom-call(f32[2]{0:T(128)S(1)} %get-tuple-element.10.factor, bf16[1,512,512]{2,1,0:T(8,128)(2,1)S(1)} %copy.20.a_ref, bf16[1,512,512]{2,1,0:T(8,128)(2,1)S(1)} %copy.21.b_ref), custom_call_target="tpu_custom_call" | custom-call | tf_op jit(solution)/shard_map/cond/branch_1_fun/far/pallas_call | solution.py:399
  299.0 0.8 copy.22
  299.8 0.8 copy.23
  (3 shorter events, 0.1 us)

commit v2 on v1

v2 whole, which is shorter than its diff:
```python
import functools

import jax
import jax.numpy as jnp
from jax import lax
from jax.experimental import pallas as pl
from jax.experimental.pallas import tpu as pltpu
from jax.sharding import PartitionSpec as P

D = 8192
KV = 512
ROUNDS = 4
MIXES = (0.5, 0.4, 0.3, 0.2)
MESH = pl.DeviceIdType.MESH
F32 = jnp.float32
BF16 = jnp.bfloat16

CHIPS = 8
DEVS = 16
TOK = 128
ROWS = 512
HALF = KV // 2
QW = 128
ITEM = 256
NT = DEVS * TOK // ITEM
NQ = HALF // QW
NOWN = NT * NQ
NITEM = 2 * NOWN
SKEW = 4
MARGIN = 2
LATE = 1
GAP = 4

ORDERS = (("y", 0), ("y", 1), ("x", 0), ("x", 1))
BITS = {"y": (1, 3), "x": (8, 24)}
LEVELS = {"y": (0, 1), "x": (3, 4)}
FAR_LEVEL = 2


def blocks(rows, step, body):
    def one(i, carry):
        body(pl.ds(pl.multiple_of(i * step, step), step))
        return carry

    lax.fori_loop(0, rows // step, one, 0)


class Mix:
    def __init__(self, raw, acc, send, recv, ssem, rsem, coef, step):
        self.raw, self.acc, self.send, self.recv = raw, acc, send, recv
        self.ssem, self.rsem, self.coef, self.step = ssem, rsem, coef, step
        self.size = raw.shape[0] // 4

    def axis_of(self, k, stage):
        first, order = ORDERS[k]
        axis = first if stage < 2 else ("x" if first == "y" else "y")
        return axis, order

    def factors(self, k, stage):
        axis, order = self.axis_of(k, stage)
        (a0, b0), (a1, b1) = (self.coef[level] for level in LEVELS[axis])
        if order == 0:
            return b0 * b1, a0 * b1, a0 * a1, b0 * a1
        return b0 * a1, a0 * b1, a0 * a1, b0 * b1

    def copy(self, k, stage):
        axis, order = self.axis_of(k, stage)
        bit = BITS[axis][order if stage % 2 == 0 else 1 - order]
        rows = pl.ds(k * self.size, self.size)
        src = self.raw.at[rows] if stage == 0 else self.send.at[stage - 1, rows]
        return pltpu.make_async_remote_copy(
            src_ref=src,
            dst_ref=self.recv.at[stage, rows],
            send_sem=self.ssem.at[k, stage],
            recv_sem=self.rsem.at[k, stage],
            device_id={"group": lax.axis_index("group") ^ bit},
            device_id_type=MESH,
        )

    def begin(self, k):
        self.copy(k, 0).start()

    def advance(self, k, stage):
        self.copy(k, stage - 1).wait_recv()
        if stage in (1, 3):
            s_own, s_got, o_own, o_got = self.factors(k, stage)

        def body(rows):
            at = pl.ds(k * self.size + rows.start, self.step)
            got = self.recv[stage - 1, at].astype(F32)
            if stage == 1:
                own = self.raw[at].astype(F32)
            else:
                own = self.acc[at]
            if stage in (1, 3):
                self.send[stage - 1, at] = (s_own * own + s_got * got).astype(BF16)
                self.acc[at] = o_own * own + o_got * got
            else:
                total = own + got
                self.acc[at] = total
                if stage == 2:
                    self.send[1, at] = total.astype(BF16)

        blocks(self.size, self.step, body)
        if stage < 4:
            self.copy(k, stage).start()

    def drain(self):
        for k in range(4):
            for stage in range(4):
                self.copy(k, stage).wait_send()


def level_factors(exponent, level):
    left = jnp.float32(1.0)
    for rnd in range(ROUNDS):
        left = left * jnp.where(exponent[rnd] == level, jnp.float32(1.0 - 2.0 * MIXES[rnd]), jnp.float32(1.0))
    return (1.0 + left) * 0.5, (1.0 - left) * 0.5


def step_kernel(
    with_far, exponent, inputs, teacher, weight, momentum, out_w, out_m,
    xc, wm, wc, tc, wm_acc, wm_send, wm_recv, part, flow_in, flow_out, cross_in, err,
    g_raw, g_acc, g_send, g_recv, fin, far_out, far_in,
    a2a_s, a2a_r, fwd_s, fwd_r, own_s, sib_s, sib_r, wm_ss, wm_rs, g0_ss, g0_rs, g1_ss, g1_rs,
    flow_s, flow_r, cross_s, cross_r, fin_l, fin_s, fin_r, far_s, far_r,
):
    group, f = lax.axis_index("group"), lax.axis_index("fsdp")
    z, c = f // 2, f % 2
    scale = D ** (-0.5)
    coef = {level: level_factors(exponent, level) for level in range(5)}

    barrier = pltpu.get_barrier_semaphore()

    def greet(i, carry):
        pl.semaphore_signal(
            barrier, inc=1, device_id={"fsdp": (f + i) % DEVS}, device_id_type=MESH
        )
        return carry

    lax.fori_loop(1, DEVS, greet, 0)
    bits = BITS["y"] + BITS["x"] + ((4,) if with_far else ())
    for bit in bits:
        pl.semaphore_signal(
            barrier, inc=1, device_id={"group": group ^ bit}, device_id_type=MESH
        )
    pl.semaphore_wait(barrier, DEVS - 1 + len(bits))

    def to_sibling(src, dst, s, r):
        return pltpu.make_async_remote_copy(
            src_ref=src, dst_ref=dst, send_sem=s, recv_sem=r,
            device_id={"fsdp": f ^ 1}, device_id_type=MESH,
        )

    def far_device(i, ahead):
        return (z + ahead) % CHIPS * 2 + i % 2

    def block(i, there):
        dev = far_device(i, i // 2 if there else CHIPS - i // 2)
        to = dev if there else f
        of = f if there else dev
        return dev, pltpu.make_async_remote_copy(
            src_ref=inputs.at[0, :, pl.ds(pl.multiple_of(to * ROWS, ROWS), ROWS)],
            dst_ref=xc.at[
                pl.ds(pl.multiple_of(of * TOK, TOK), TOK),
                pl.ds(pl.multiple_of((to % 2) * ROWS, ROWS), ROWS),
            ],
            send_sem=a2a_s.at[i],
            recv_sem=a2a_r.at[of],
            device_id={"fsdp": dev},
            device_id_type=MESH,
        )

    def send_block(i, carry):
        block(i, True)[1].start()
        return carry

    lax.fori_loop(2, DEVS, send_block, 0)

    mine = pl.ds(pl.multiple_of(c * HALF, HALF), HALF)
    other = pl.ds(pl.multiple_of((1 - c) * HALF, HALF), HALF)
    every = pl.ds(0, KV)
    w_rows = pl.ds(pl.multiple_of(c * ROWS, ROWS), ROWS)
    m_rows = pl.ds(pl.multiple_of(2 * ROWS + c * ROWS, ROWS), ROWS)
    t_rows = pl.ds(pl.multiple_of(c * TOK, TOK), TOK)
    x_rows = pl.ds(pl.multiple_of(f * TOK, TOK), TOK)
    x_cols = pl.ds(pl.multiple_of(z * 2 * ROWS, 2 * ROWS), 2 * ROWS)
    shared = (
        (weight, mine, other, wm, w_rows),
        (momentum, mine, other, wm, m_rows),
        (weight, every, every, wc, w_rows),
        (teacher, every, every, tc, t_rows),
        (inputs, x_cols, x_cols, xc, x_rows),
    )
    local = [
        pltpu.make_async_copy(src.at[0, :, keep], dst.at[rows], own_s.at[i])
        for i, (src, keep, _, dst, rows) in enumerate(shared)
    ]
    across = [
        to_sibling(src.at[0, :, give], dst.at[rows], sib_s.at[i], sib_r.at[i])
        for i, (src, _, give, dst, rows) in enumerate(shared)
    ]
    for i in range(5):
        local[i].start()
        across[i].start()

    def zeros(ref):
        ref[...] = jnp.zeros_like(ref)

    place = jnp.where(c == 0, z, CHIPS - 1 - z)
    pl.when(place == 0)(lambda: zeros(flow_in))
    pl.when(place == CHIPS - 1)(lambda: zeros(cross_in))

    for i in range(2):
        local[i].wait()
        across[i].wait()
    mix = Mix(wm, wm_acc, wm_send, wm_recv, wm_ss, wm_rs, coef, 64)
    for k in range(4):
        mix.begin(k)
    for stage in range(1, 5):
        for k in range(4):
            mix.advance(k, stage)
    mix.drain()

    def to_far(i):
        return pltpu.make_async_remote_copy(
            src_ref=far_out.at[i], dst_ref=far_in.at[i], send_sem=far_s.at[i], recv_sem=far_r.at[i],
            device_id={"group": group ^ 4}, device_id_type=MESH,
        )

    if with_far:

        def w_out(rows):
            for q in range(NQ):
                far_out[NQ + q, rows] = wm_acc[rows, q * QW : (q + 1) * QW].astype(BF16)

        blocks(2 * ROWS, 64, w_out)

    def item_of(q, core, t):
        return (q * 2 + core) * NT + t

    def share(chip):
        rows = pl.ds(pl.multiple_of(chip * ITEM, ITEM), ITEM)
        own = jnp.dot(xc[rows], wc[...], preferred_element_type=F32) * scale
        for core in range(2):
            for q in range(NQ):
                at = core * HALF + q * QW
                part[item_of(q, core, chip)] = own[:, at : at + QW]

    for i in range(2, 5):
        local[i].wait()
        across[i].wait()
    share(z)
    for core in range(2):
        for q in range(NQ):
            at = core * HALF + q * QW
            n = item_of(q, core, z)
            part[n] = part[n] - tc[:, at : at + QW].astype(F32)

    def forward(j, cols):
        at = (pl.ds(pl.multiple_of(j * TOK, TOK), TOK), pl.ds(pl.multiple_of(cols * ROWS, ROWS), ROWS))
        return to_sibling(xc.at[at], xc.at[at], fwd_s.at[j], fwd_r.at[j])

    def pass_on(ahead):
        for i in range(2):
            dev, arrival = block(2 * ahead + i, False)
            arrival.wait_recv()
            forward(dev, c).start()

    def settle(ahead):
        for i in range(2):
            dev = far_device(i, CHIPS - ahead)
            forward(dev, c).wait_send()
            forward(dev, 1 - c).wait_recv()
            block(2 * ahead + i, True)[1].wait_send()
        share((z + CHIPS - ahead) % CHIPS)

    def arrive(ahead, carry):
        pass_on(ahead)
        pl.when(ahead > 1)(lambda: settle(ahead - 1))
        return carry

    lax.fori_loop(1, CHIPS, arrive, 0)
    settle(CHIPS - 1)
    def hop(n):
        return pltpu.make_async_remote_copy(
            src_ref=flow_out.at[n], dst_ref=flow_in.at[n], send_sem=flow_s.at[n], recv_sem=flow_r.at[n],
            device_id={"fsdp": (f + DEVS + 2 - 4 * c) % DEVS}, device_id_type=MESH,
        )

    def cross(m, n):
        return to_sibling(flow_in.at[n], cross_in.at[m], cross_s.at[m], cross_r.at[m])

    sems = ((g0_ss, g0_rs), (g1_ss, g1_rs))
    mixes = [
        Mix(g_raw.at[q], g_acc.at[q], g_send.at[q], g_recv.at[q], *sems[q], coef, 256) for q in range(NQ)
    ]

    def grad(q):
        turned = err[q * NT : (q + 1) * NT].reshape(DEVS * TOK, QW).T
        for k in range(4):
            size = 2 * ROWS // 4
            got = jnp.dot(turned, xc[:, k * size : (k + 1) * size], preferred_element_type=F32)
            g_raw[q, k * size : (k + 1) * size] = (got * scale).T.astype(BF16)
            mixes[q].begin(k)

    def advance(q, stage):
        for k in range(4):
            mixes[q].advance(k, stage)

    def moved_of(q, rows):
        cols = slice(q * QW, (q + 1) * QW)
        return 0.9 * wm_acc[pl.ds(2 * ROWS + rows.start, 64), cols] + g_acc[q, rows]

    out_cols = [pl.ds(pl.multiple_of(c * HALF + q * QW, QW), QW) for q in range(NQ)]
    o_rows = pl.ds(pl.multiple_of((1 - c) * ROWS, ROWS), ROWS)

    def ends(q):
        copies = []
        for i, out in enumerate((out_w, out_m)):
            at = out.at[0, :, out_cols[q]]
            k = 2 * q + i
            copies.append(to_sibling(fin.at[k, o_rows], at, fin_s.at[k], fin_r.at[k]))
            copies.append(pltpu.make_async_copy(fin.at[k, w_rows], at, fin_l.at[k]))
        return copies

    def mixed(q):
        if with_far:

            def body(rows):
                far_out[q, rows] = moved_of(q, rows).astype(BF16)

            blocks(2 * ROWS, 64, body)
            to_far(q).start()
        else:

            def body(rows):
                moved = moved_of(q, rows)
                fin[2 * q + 1, rows] = moved.astype(BF16)
                fin[2 * q, rows] = (wm_acc[rows, q * QW : (q + 1) * QW] - 0.05 * moved).astype(BF16)

            blocks(2 * ROWS, 64, body)
            for copy in ends(q):
                copy.start()

    def finish(q):
        if with_far:
            own, far = coef[FAR_LEVEL]
            to_far(NQ + q).wait()
            to_far(q).wait()

            def body(rows):
                moved = own * moved_of(q, rows) + far * far_in[q, rows].astype(F32)
                kept = own * wm_acc[rows, q * QW : (q + 1) * QW] + far * far_in[NQ + q, rows].astype(F32)
                fin[2 * q + 1, rows] = moved.astype(BF16)
                fin[2 * q, rows] = (kept - 0.05 * moved).astype(BF16)

            blocks(2 * ROWS, 64, body)
            for copy in ends(q):
                copy.start()

    def own_index(n):
        return n // (2 * NT) * NT + n % NT

    lag = SKEW * jnp.maximum(CHIPS - 1 - 2 * place, 0) + MARGIN
    late = jnp.logical_and(place > LATE, place < CHIPS - 1 - LATE)

    def step(s, carry):
        @pl.when(s < NITEM)
        def _():
            @pl.when(place > 0)
            def _():
                hop(s).wait_recv()

            @pl.when(place < CHIPS - 1)
            def _():
                flow_out[s] = (part[s] + flow_in[s].astype(F32)).astype(BF16)
                hop(s).start()

            @pl.when(jnp.logical_and(place > 0, s // NT % 2 != c))
            def _():
                cross(own_index(s), s).start()

        n = s - lag

        @pl.when(jnp.logical_and(jnp.logical_and(n >= 0, n < NITEM), n // NT % 2 == c))
        def _():
            m = own_index(n)

            @pl.when(place < CHIPS - 1)
            def _():
                cross(m, n).wait_recv()

            err[m] = (part[n] + flow_in[n].astype(F32) + cross_in[m].astype(F32)).astype(BF16)

        @pl.when(jnp.logical_not(late))
        def _():
            pl.when(n == 2 * NT)(lambda: grad(0))
            for stage in range(1, 5):
                pl.when(n == 2 * NT + GAP * stage)(lambda stage=stage: advance(0, stage))

        return carry

    steps = max(NITEM, 2 * NT + 4 * GAP + 1)
    lax.fori_loop(0, steps + SKEW * (CHIPS - 1) + MARGIN, step, 0)

    pl.when(late)(lambda: grad(0))
    grad(1)
    if with_far:
        for q in range(NQ):
            to_far(NQ + q).start()

    pl.when(jnp.logical_not(late))(lambda: mixed(0))
    for stage in range(1, 5):
        pl.when(late)(lambda stage=stage: advance(0, stage))
        advance(1, stage)
    pl.when(late)(lambda: mixed(0))
    mixed(1)

    def sent(n, carry):
        pl.when(place < CHIPS - 1)(lambda: hop(n).wait_send())
        pl.when(jnp.logical_and(place > 0, n // NT % 2 != c))(lambda: cross(own_index(n), n).wait_send())
        return carry

    lax.fori_loop(0, NITEM, sent, 0)
    for q in range(NQ):
        mixes[q].drain()
    for q in range(NQ):
        finish(q)
    for q in range(NQ):
        for copy in ends(q):
            copy.wait()


def step_call(with_far, exponent, inputs, teacher, weight, momentum):
    dma = lambda *n: pltpu.SemaphoreType.DMA(n)
    anywhere = pl.BlockSpec(memory_space=pl.ANY)
    shape = jax.ShapeDtypeStruct((1, ROWS, KV), BF16)
    rows = 2 * ROWS
    far = 2 * NQ
    return pl.pallas_call(
        functools.partial(step_kernel, with_far),
        name="step_far" if with_far else "step_near",
        out_shape=(shape, shape),
        in_specs=[pl.BlockSpec(memory_space=pltpu.SMEM)] + [anywhere] * 4,
        out_specs=(anywhere, anywhere),
        scratch_shapes=[
            pltpu.VMEM((DEVS * TOK, rows), BF16),
            pltpu.VMEM((2 * rows, HALF), BF16),
            pltpu.VMEM((rows, KV), BF16),
            pltpu.VMEM((2 * TOK, KV), BF16),
            pltpu.VMEM((2 * rows, HALF), F32),
            pltpu.VMEM((3, 2 * rows, HALF), BF16),
            pltpu.VMEM((4, 2 * rows, HALF), BF16),
            pltpu.VMEM((NITEM, ITEM, QW), F32),
            pltpu.VMEM((NITEM, ITEM, QW), BF16),
            pltpu.VMEM((NITEM, ITEM, QW), BF16),
            pltpu.VMEM((NOWN, ITEM, QW), BF16),
            pltpu.VMEM((NOWN, ITEM, QW), BF16),
            pltpu.VMEM((NQ, rows, QW), BF16),
            pltpu.VMEM((NQ, rows, QW), F32),
            pltpu.VMEM((NQ, 3, rows, QW), BF16),
            pltpu.VMEM((NQ, 4, rows, QW), BF16),
            pltpu.VMEM((2 * NQ, rows, QW), BF16),
            pltpu.VMEM((far, rows, QW), BF16),
            pltpu.VMEM((far, rows, QW), BF16),
            dma(DEVS), dma(DEVS), dma(DEVS), dma(DEVS),
            dma(5), dma(5), dma(5),
            dma(4, 4), dma(4, 4), dma(4, 4), dma(4, 4), dma(4, 4), dma(4, 4),
            dma(NITEM), dma(NITEM), dma(NOWN), dma(NOWN),
            dma(2 * NQ), dma(2 * NQ), dma(2 * NQ),
            dma(far), dma(far),
        ],
        compiler_params=pltpu.CompilerParams(
            collective_id=int(with_far), has_side_effects=True, vmem_limit_bytes=56 * 2**20
        ),
    )(exponent, inputs, teacher, weight, momentum)


def per_device(inputs, teacher, weight, momentum, exponent):
    return lax.cond(
        jnp.any(exponent == FAR_LEVEL),
        lambda *args: tuple(step_call(True, *args)),
        lambda *args: tuple(step_call(False, *args)),
        exponent, inputs, teacher, weight, momentum,
    )


def solution(mesh):
    return jax.shard_map(
        per_device,
        mesh=mesh,
        in_specs=(
            P("group", "fsdp", None),
            P("group", "fsdp", None),
            P("group", "fsdp", None),
            P("group", "fsdp", None),
            P(),
        ),
        out_specs=(P("group", "fsdp", None), P("group", "fsdp", None)),
        check_vma=False,
    )
```

time: 301 us -> 185 us (0.61)
  the two profiles are of different devices: /device:TPU:65 before, /device:TPU:1 now
where the time goes in v2:
time: 185 us
  Pallas kernels  180 us (97%)
    pallas_call x1, Pallas kernels, step_call(): pl.pallas_call(functools.partial(step_kernel, with_far), name='step_far'...  180 us

profile of v2, /device:TPU:1, one launch (start us, length us, event | category | flops | bytes accessed | tf_op | source)
XLA Modules:
  0.0 184.5 jit_solution(645612881497318399)
XLA Ops:
  0.6 1.3 compare_reduce_fusion
  2.6 180.3 %conditional.1 = ((bf16[1,512,512]{2,1,0:T(8,128)(2,1)S(1)}, bf16[1,512,512]{2,1,0:T(8,128)(2,1)S(1)})) conditional(s32[]{:T(128)} %convert_element_type.3, (s32[4]{0:T(128)}, bf16[1,128,8192]{2,1,0:T(8,128)(2,1)}, bf16[1,128,512]{2,1,0:T(8,128)(2,1)}, bf16[1,512,512]{2,1,0:T(8,128)(2,1)}, bf16[1,512,512]{2,1,0:T(8,128)(2,1)}) %tuple.13, ...), branch_computations={%region_1.0_spmd, %region_2.0_spmd} | conditional | bytes 8 | solution.py:481
  2.6 180.1 %step_near.1 = (bf16[1,512,512]{2,1,0:T(8,128)(2,1)S(1)}, bf16[1,512,512]{2,1,0:T(8,128)(2,1)S(1)}) custom-call(s32[4]{0:T(128)} %get-tuple-element.20.exponent, bf16[1,128,8192]{2,1,0:T(8,128)(2,1)} %get-tuple-element.46.inputs, bf16[1,128,512]{2,1,0:T(8,128)(2,1)} %get-tuple-element.48.teacher, bf16[1,512,512]{2,1,0:T(8,128)(2,1)} %get-tuple-element.50.weight, ...), custom_call_target="tpu_custom_call" | custom-call | tf_op jit(solution)/shard_map/cond/branch_0_fun/step_near/pallas_call | solution.py:441
  182.9 0.8 copy.25
  183.7 0.8 copy.26

commit v3 on v2

--- a/solution.py
+++ b/solution.py
@@ -35,6 +35,9 @@
 BITS = {"y": (1, 3), "x": (8, 24)}
 LEVELS = {"y": (0, 1), "x": (3, 4)}
 FAR_LEVEL = 2
+NEAR, FAR_WHOLE, FAR_HALF = range(3)
+SHARE_LEVELS = (0, 1, 3, 4)
+PIECE = 256
 
 
 def blocks(rows, step, body):
@@ -119,11 +122,11 @@
 
 
 def step_kernel(
-    with_far, exponent, inputs, teacher, weight, momentum, out_w, out_m,
+    mode, exponent, inputs, teacher, weight, momentum, out_w, out_m,
     xc, wm, wc, tc, wm_acc, wm_send, wm_recv, part, flow_in, flow_out, cross_in, err,
-    g_raw, g_acc, g_send, g_recv, fin, far_out, far_in,
+    g_raw, g_acc, g_send, g_recv, fin, far_out, far_in, share_in,
     a2a_s, a2a_r, fwd_s, fwd_r, own_s, sib_s, sib_r, wm_ss, wm_rs, g0_ss, g0_rs, g1_ss, g1_rs,
-    flow_s, flow_r, cross_s, cross_r, fin_l, fin_s, fin_r, far_s, far_r,
+    flow_s, flow_r, cross_s, cross_r, fin_l, fin_s, fin_r, far_s, far_r, share_s, share_r,
 ):
     group, f = lax.axis_index("group"), lax.axis_index("fsdp")
     z, c = f // 2, f % 2
@@ -139,7 +142,8 @@
         return carry
 
     lax.fori_loop(1, DEVS, greet, 0)
-    bits = BITS["y"] + BITS["x"] + ((4,) if with_far else ())
+    with_far = mode != NEAR
+    bits = BITS["y"] + BITS["x"] + ((4,) if with_far else ()) + ((2, 16) if mode == FAR_HALF else ())
     for bit in bits:
         pl.semaphore_signal(
             barrier, inc=1, device_id={"group": group ^ bit}, device_id_type=MESH
@@ -222,11 +226,36 @@
             mix.advance(k, stage)
     mix.drain()
 
-    def to_far(i):
+    half = (group + group // 2 + group // 8 + group // 16) % 2
+    first_row = half * ROWS if mode == FAR_HALF else 0
+    pieces = (ROWS if mode == FAR_HALF else 2 * ROWS) // PIECE
+
+    def to_far(i, p):
+        rows = pl.ds(pl.multiple_of(first_row + p * PIECE, PIECE), PIECE)
         return pltpu.make_async_remote_copy(
-            src_ref=far_out.at[i], dst_ref=far_in.at[i], send_sem=far_s.at[i], recv_sem=far_r.at[i],
+            src_ref=far_out.at[i, rows], dst_ref=far_in.at[i, rows],
+            send_sem=far_s.at[i, p], recv_sem=far_r.at[i, p],
             device_id={"group": group ^ 4}, device_id_type=MESH,
         )
+
+    def send_far(i):
+        for p in range(pieces):
+            to_far(i, p).start()
+
+    def to_share(i, p, k):
+        rows = pl.ds(pl.multiple_of(first_row + p * PIECE, PIECE), PIECE)
+        return pltpu.make_async_remote_copy(
+            src_ref=far_in.at[i, rows], dst_ref=share_in.at[k, i, pl.ds(p * PIECE, PIECE)],
+            send_sem=share_s.at[k, i, p], recv_sem=share_r.at[k, i, p],
+            device_id={"group": group ^ (1 << SHARE_LEVELS[k])}, device_id_type=MESH,
+        )
+
+    def hand_on(i):
+        for p in range(pieces):
+            to_far(i, p).wait_recv()
+            if mode == FAR_HALF:
+                for k in range(len(SHARE_LEVELS)):
+                    to_share(i, p, k).start()
 
     if with_far:
 
@@ -282,6 +311,10 @@
 
     lax.fori_loop(1, CHIPS, arrive, 0)
     settle(CHIPS - 1)
+    if with_far:
+        for q in range(NQ):
+            send_far(NQ + q)
+
     def hop(n):
         return pltpu.make_async_remote_copy(
             src_ref=flow_out.at[n], dst_ref=flow_in.at[n], send_sem=flow_s.at[n], recv_sem=flow_r.at[n],
@@ -331,7 +364,7 @@
                 far_out[q, rows] = moved_of(q, rows).astype(BF16)
 
             blocks(2 * ROWS, 64, body)
-            to_far(q).start()
+            send_far(q)
         else:
 
             def body(rows):
@@ -346,16 +379,35 @@
     def finish(q):
         if with_far:
             own, far = coef[FAR_LEVEL]
-            to_far(NQ + q).wait()
-            to_far(q).wait()
-
-            def body(rows):
-                moved = own * moved_of(q, rows) + far * far_in[q, rows].astype(F32)
-                kept = own * wm_acc[rows, q * QW : (q + 1) * QW] + far * far_in[NQ + q, rows].astype(F32)
+            if mode == FAR_HALF:
+                for i in (NQ + q, q):
+                    for p in range(pieces):
+                        for k in range(len(SHARE_LEVELS)):
+                            to_share(i, p, k).wait_recv()
+
+            def shared_far(i, at):
+                got = share_in[0, i, at]
+                for k in range(1, len(SHARE_LEVELS)):
+                    got = jnp.where(exponent[0] == SHARE_LEVELS[k], share_in[k, i, at], got)
+                return got.astype(F32)
+
+            def end(rows, far_of):
+                moved = own * moved_of(q, rows) + far * far_of(q)
+                kept = own * wm_acc[rows, q * QW : (q + 1) * QW] + far * far_of(NQ + q)
                 fin[2 * q + 1, rows] = moved.astype(BF16)
                 fin[2 * q, rows] = (kept - 0.05 * moved).astype(BF16)
 
-            blocks(2 * ROWS, 64, body)
+            def direct(at):
+                rows = pl.ds(pl.multiple_of(first_row + at.start, 64), 64)
+                end(rows, lambda i: far_in[i, rows].astype(F32))
+
+            def handed(at):
+                rows = pl.ds(pl.multiple_of((1 - half) * ROWS + at.start, 64), 64)
+                end(rows, lambda i: shared_far(i, at))
+
+            blocks(pieces * PIECE, 64, direct)
+            if mode == FAR_HALF:
+                blocks(ROWS, 64, handed)
             for copy in ends(q):
                 copy.start()
 
@@ -406,10 +458,6 @@
 
     pl.when(late)(lambda: grad(0))
     grad(1)
-    if with_far:
-        for q in range(NQ):
-            to_far(NQ + q).start()
-
     pl.when(jnp.logical_not(late))(lambda: mixed(0))
     for stage in range(1, 5):
         pl.when(late)(lambda stage=stage: advance(0, stage))
@@ -425,22 +473,34 @@
     lax.fori_loop(0, NITEM, sent, 0)
     for q in range(NQ):
         mixes[q].drain()
+    if with_far:
+        for q in range(NQ):
+            hand_on(NQ + q)
+        for q in range(NQ):
+            hand_on(q)
     for q in range(NQ):
         finish(q)
+    if with_far:
+        for i in range(2 * NQ):
+            for p in range(pieces):
+                to_far(i, p).wait_send()
+                if mode == FAR_HALF:
+                    for k in range(len(SHARE_LEVELS)):
+                        to_share(i, p, k).wait_send()
     for q in range(NQ):
         for copy in ends(q):
             copy.wait()
 
 
-def step_call(with_far, exponent, inputs, teacher, weight, momentum):
+def step_call(mode, exponent, inputs, teacher, weight, momentum):
     dma = lambda *n: pltpu.SemaphoreType.DMA(n)
     anywhere = pl.BlockSpec(memory_space=pl.ANY)
     shape = jax.ShapeDtypeStruct((1, ROWS, KV), BF16)
     rows = 2 * ROWS
     far = 2 * NQ
     return pl.pallas_call(
-        functools.partial(step_kernel, with_far),
-        name="step_far" if with_far else "step_near",
+        functools.partial(step_kernel, mode),
+        name=("step_near", "step_far_whole", "step_far_half")[mode],
         out_shape=(shape, shape),
         in_specs=[pl.BlockSpec(memory_space=pltpu.SMEM)] + [anywhere] * 4,
         out_specs=(anywhere, anywhere),
@@ -464,24 +524,26 @@
             pltpu.VMEM((2 * NQ, rows, QW), BF16),
             pltpu.VMEM((far, rows, QW), BF16),
             pltpu.VMEM((far, rows, QW), BF16),
+            pltpu.VMEM((len(SHARE_LEVELS), far, ROWS, QW), BF16),
             dma(DEVS), dma(DEVS), dma(DEVS), dma(DEVS),
             dma(5), dma(5), dma(5),
             dma(4, 4), dma(4, 4), dma(4, 4), dma(4, 4), dma(4, 4), dma(4, 4),
             dma(NITEM), dma(NITEM), dma(NOWN), dma(NOWN),
             dma(2 * NQ), dma(2 * NQ), dma(2 * NQ),
-            dma(far), dma(far),
+            dma(far, rows // PIECE), dma(far, rows // PIECE),
+            dma(len(SHARE_LEVELS), far, ROWS // PIECE), dma(len(SHARE_LEVELS), far, ROWS // PIECE),
         ],
         compiler_params=pltpu.CompilerParams(
-            collective_id=int(with_far), has_side_effects=True, vmem_limit_bytes=56 * 2**20
+            collective_id=mode, has_side_effects=True, vmem_limit_bytes=56 * 2**20
         ),
     )(exponent, inputs, teacher, weight, momentum)
 
 
 def per_device(inputs, teacher, weight, momentum, exponent):
-    return lax.cond(
-        jnp.any(exponent == FAR_LEVEL),
-        lambda *args: tuple(step_call(True, *args)),
-        lambda *args: tuple(step_call(False, *args)),
+    far = jnp.where(exponent[0] == FAR_LEVEL, FAR_WHOLE, FAR_HALF)
+    return lax.switch(
+        jnp.where(jnp.any(exponent == FAR_LEVEL), far, NEAR),
+        [lambda *args, mode=mode: tuple(step_call(mode, *args)) for mode in (NEAR, FAR_WHOLE, FAR_HALF)],
         exponent, inputs, teacher, weight, momentum,
     )
 

time: 185 us -> 237 us (1.28)
  Pallas kernels: 180 us -> 232 us
    pallas_call x1, Pallas kernels: 180 us -> 232 us  [step_call(): pl.pallas_call(functools.partial(step_kernel, mode), name=('step_near', '...]
where the time goes in v3:
time: 237 us
  Pallas kernels  232 us (98%)
    pallas_call x1, Pallas kernels, step_call(): pl.pallas_call(functools.partial(step_kernel, mode), name=('step_near', '...  232 us

profile of v3, /device:TPU:1, one launch (start us, length us, event | category | flops | bytes accessed | tf_op | source)
XLA Modules:
  0.0 237.1 jit_solution(4372897142569986504)
XLA Ops:
  0.6 1.3 compare_reduce_fusion
  3.2 232.3 %conditional.1 = ((bf16[1,512,512]{2,1,0:T(8,128)(2,1)S(1)}, bf16[1,512,512]{2,1,0:T(8,128)(2,1)S(1)})) conditional(s32[]{:T(128)} %clamp.3, (s32[4]{0:T(128)}, bf16[1,128,8192]{2,1,0:T(8,128)(2,1)}, bf16[1,128,512]{2,1,0:T(8,128)(2,1)}, bf16[1,512,512]{2,1,0:T(8,128)(2,1)}, bf16[1,512,512]{2,1,0:T(8,128)(2,1)}) %tuple.16, ...), branch_computations={%region_1.2_spmd, %region_2.3_spmd, %region_3.4_spmd} | conditional | bytes 8 | solution.py:544
  3.5 231.8 %step_far_half.1 = (bf16[1,512,512]{2,1,0:T(8,128)(2,1)S(1)}, bf16[1,512,512]{2,1,0:T(8,128)(2,1)S(1)}) custom-call(s32[4]{0:T(128)} %get-tuple-element.40.exponent, bf16[1,128,8192]{2,1,0:T(8,128)(2,1)} %get-tuple-element.41.inputs, bf16[1,128,512]{2,1,0:T(8,128)(2,1)} %get-tuple-element.42.teacher, bf16[1,512,512]{2,1,0:T(8,128)(2,1)} %get-tuple-element.43.weight, ...), custom_call_target="tpu_custom_call" | custom-call | tf_op jit(solution)/shard_map/cond/branch_2_fun/step_far_half/pallas_call | solution.py:501
  235.5 0.8 copy.21
  236.3 0.8 copy.22

commit v4 on v3

--- a/solution.py
+++ b/solution.py
@@ -476,9 +476,9 @@
     if with_far:
         for q in range(NQ):
             hand_on(NQ + q)
-        for q in range(NQ):
+    for q in range(NQ):
+        if with_far:
             hand_on(q)
-    for q in range(NQ):
         finish(q)
     if with_far:
         for i in range(2 * NQ):

time: 237 us -> 186 us (0.78)
  Pallas kernels: 232 us -> 181 us
    pallas_call x1, Pallas kernels: 232 us -> 181 us  [step_call(): pl.pallas_call(functools.partial(step_kernel, mode), name=('step_near', '...]
where the time goes in v4:
time: 186 us
  Pallas kernels  181 us (97%)
  between operations  1.94 us (1%)
    pallas_call x1, Pallas kernels, step_call(): pl.pallas_call(functools.partial(step_kernel, mode), name=('step_near', '...  181 us

profile of v4, /device:TPU:1, one launch (start us, length us, event | category | flops | bytes accessed | tf_op | source)
XLA Modules:
  0.0 186.0 jit_solution(17472172421053227557)
XLA Ops:
  0.6 1.3 compare_reduce_fusion
  3.2 181.2 %conditional.1 = ((bf16[1,512,512]{2,1,0:T(8,128)(2,1)S(1)}, bf16[1,512,512]{2,1,0:T(8,128)(2,1)S(1)})) conditional(s32[]{:T(128)} %clamp.3, (s32[4]{0:T(128)}, bf16[1,128,8192]{2,1,0:T(8,128)(2,1)}, bf16[1,128,512]{2,1,0:T(8,128)(2,1)}, bf16[1,512,512]{2,1,0:T(8,128)(2,1)}, bf16[1,512,512]{2,1,0:T(8,128)(2,1)}) %tuple.16, ...), branch_computations={%region_1.2_spmd, %region_2.3_spmd, %region_3.4_spmd} | conditional | bytes 8 | solution.py:544
  3.2 180.9 %step_near.1 = (bf16[1,512,512]{2,1,0:T(8,128)(2,1)S(1)}, bf16[1,512,512]{2,1,0:T(8,128)(2,1)S(1)}) custom-call(s32[4]{0:T(128)} %get-tuple-element.30.exponent, bf16[1,128,8192]{2,1,0:T(8,128)(2,1)} %get-tuple-element.31.inputs, bf16[1,128,512]{2,1,0:T(8,128)(2,1)} %get-tuple-element.32.teacher, bf16[1,512,512]{2,1,0:T(8,128)(2,1)} %get-tuple-element.33.weight, ...), custom_call_target="tpu_custom_call" | custom-call | tf_op jit(solution)/shard_map/cond/branch_0_fun/step_near/pallas_call | solution.py:501
  184.4 0.8 copy.21
  185.2 0.8 copy.22
